TPU v7x, 128 devices: a whole 4x4x4 slice. The times are simulated.
128 devices in a mesh: cluster: 8 (over z, x_hi), dp: 16 (over y, x_lo, core).
Axes of the slice: x: 4 (x_hi: 2, x_lo: 2; x = x_hi * 2 + x_lo), y: 4, z: 4, core: 2. Of those that a mesh axis runs over, the one named last changes fastest.
Arguments:
- documents: bfloat16 [32768, 1024], P('dp', 'cluster'), may hold values from -64 to 64
- centroids: bfloat16 [16384, 1024], P('cluster'), may hold values from -8 to 8
- domain_mass: float32 [32768, 256], P('dp'), may hold values from 0.01 to 10
Outputs:
- lift: float32 [16384, 256], P(('cluster', 'dp'))
- information: float32 [], replicated
All inputs are finite; a program needn't handle non-finite values.
Results may differ from a plain program's by a relative error of at most 0.0013.
Values may be sent and summed in bfloat16 or wider, within the bound.
A program may use at most 128 MiB of HBM per device.

v0:
```python
import math
import jax
import jax.numpy as jnp
from jax import lax
from jax.sharding import PartitionSpec as P

E = 1024


def shards(documents, centroids, domain_mass):
    scale = 3.0 / math.sqrt(E)
    doc_rows = documents.shape[0]
    local_k = centroids.shape[0]
    docs_total = doc_rows * lax.axis_size("dp")
    own_rows = local_k // lax.axis_size("dp")
    columns = centroids
    scores = (
        lax.dot_general(
            lax.all_gather(documents, "cluster", axis=1, tiled=True),
            columns,
            (((1,), (1,)), ((), ())),
            preferred_element_type=jnp.float32,
        )
        * scale
    )
    row_max = lax.pmax(jnp.max(scores, axis=1), "cluster")
    expo = jnp.exp(scores - row_max[:, None])
    row_total = lax.psum(jnp.sum(expo, axis=1), "cluster")
    assign = (expo / row_total[:, None]).astype(jnp.bfloat16)
    shares = (domain_mass / jnp.sum(domain_mass, axis=1, keepdims=True)).astype(jnp.bfloat16)
    columns = assign
    whole = lax.psum(
        lax.dot_general(
            columns, shares, (((0,), (0,)), ((), ())), preferred_element_type=jnp.float32
        ),
        "dp",
    )
    summed = lax.dynamic_slice_in_dim(whole, lax.axis_index("dp") * own_rows, own_rows, 0)
    joint = summed / docs_total
    cluster_mass = jnp.sum(joint, axis=1)
    domain_prior = lax.psum(jnp.sum(joint, axis=0), ("cluster", "dp"))
    lift = joint / (cluster_mass[:, None] * domain_prior[None, :])
    information = lax.psum(jnp.sum(joint * jnp.log(lift)), ("cluster", "dp"))
    return (lift, information)


def solution(mesh):
    return jax.shard_map(
        shards,
        mesh=mesh,
        in_specs=(P("dp", "cluster"), P("cluster", None), P("dp", None)),
        out_specs=(P(("cluster", "dp"), None), P()),
        check_vma=False,
    )
```

profile of v0, /device:TPU:1, one launch (start us, length us, event | category | flops | bytes accessed | tf_op | source)
XLA Modules:
  0.0 423.9 jit_solution(605599507388424641)
XLA Ops:
  7.2 0.0 all-gather.2.cloned.1.call-start
  7.2 0.7 all-gather.2.cloned.1.call-update
  7.9 0.0 all-reduce.2.cloned.1.call-start
  7.9 1.9 reduce_sum.46
  9.9 77.0 %all-gather.2.cloned.1.call-done = bf16[2048,1024]{1,0:T(8,128)(2,1)} async-done(((bf16[2048,128]{1,0:T(8,128)(2,1)}), bf16[2048,1024]{1,0:T(8,128)(2,1)}) %all-gather.2.cloned.1.call-update) | async-done | bytes 4194320 | tf_op jit(solution)/shard_map/all_gather | solution.py:19
  86.9 15.1 %multiply_reduce_fusion = (f32[2048]{0:T(1024)S(1)}, f32[2048,2048]{0,1:T(8,128)}) fusion(bf16[2048,1024]{1,0:T(8,128)(2,1)} %all-gather.2.cloned.1.call-done, bf16[2048,1024]{1,0:T(8,128)(2,1)} %param.4), kind=kOutput, calls=%fused_computation.2 | convolution fusion | flops 8598321152 | bytes 25174016 | tf_op jit(solution)/shard_map/dot_general | solution.py:18
  102.0 16.6 %pmax.7 = f32[2048]{0:T(1024)S(1)} all-reduce(f32[2048]{0:T(1024)S(1)} %get-tuple-element.6), channel_id=1, replica_groups=mesh['cluster'=8,'dp'=16] {'cluster'}, use_global_device_ids=true, to_apply=%region_1.0 | all-reduce | flops 2048 | bytes 16384 | tf_op jit(solution)/shard_map/pmax | solution.py:26
  118.6 0.0 copy-start
  118.6 8.7 %fusion = f32[2048]{0:T(1024)S(1)} fusion(f32[2048,2048]{0,1:T(8,128)} %get-tuple-element.7, f32[2048]{0:T(1024)S(1)} %pmax.7), kind=kLoop, calls=%fused_computation.3 | loop fusion | flops 12580864 | bytes 16793600 | tf_op jit(solution)/shard_map/reduce_sum | solution.py:28
  127.3 18.2 %psum.28 = f32[2048]{0:T(1024)S(1)} all-reduce(f32[2048]{0:T(1024)S(1)} %fusion), channel_id=1, replica_groups=mesh['cluster'=8,'dp'=16] {'cluster'}, use_global_device_ids=true, to_apply=%region_3.0 | all-reduce | flops 2048 | bytes 16384 | tf_op jit(solution)/shard_map/psum | solution.py:28
  145.5 0.0 copy-done
  145.5 9.1 %fusion.1 = f32[2048,256]{1,0:T(8,128)} fusion(f32[2048,2048]{0,1:T(8,128)} %get-tuple-element.7, f32[2048]{0:T(1024)S(1)} %psum.28, f32[2048]{0:T(1024)S(1)} %pmax.7, f32[2048,256]{1,0:T(8,128)S(1)} %copy-done, f32[2048]{0:T(1024)S(1)} %reduce_sum.46), kind=kOutput, calls=%fused_computation.4 | convolution fusion | flops 2165309440 | bytes 20996096 | tf_op jit(solution)/shard_map/dot_general | solution.py:33
  154.6 0.0 all-reduce.2.cloned.1.call-update
  154.7 129.3 %all-reduce.2.cloned.1.call-done = f32[2048,256]{1,0:T(8,128)} async-done(((f32[2048,256]{1,0:T(8,128)}), f32[2048,256]{1,0:T(8,128)}) %all-reduce.2.cloned.1.call-update) | async-done | bytes 2097168 | tf_op jit(solution)/shard_map/psum | solution.py:32
  283.9 1.0 fusion.4
  284.9 67.3 %psum.30 = f32[256]{0:T(256)S(1)} all-reduce(f32[256]{0:T(256)S(1)} %get-tuple-element.3), channel_id=1, replica_groups=mesh['cluster'=8,'dp'=16] {'cluster','dp'}, use_global_device_ids=true, to_apply=%region_8.0 | all-reduce | flops 256 | bytes 2048 | tf_op jit(solution)/shard_map/psum | solution.py:41
  352.2 2.3 multiply_reduce_fusion.1
  354.5 62.6 %psum.31 = f32[]{:T(128)} all-reduce(f32[]{:T(128)} %get-tuple-element.4), channel_id=1, replica_groups=mesh['cluster'=8,'dp'=16] {'cluster','dp'}, use_global_device_ids=true, to_apply=%region_10.0 | all-reduce | flops 1 | bytes 8 | tf_op jit(solution)/shard_map/psum | solution.py:43
Async XLA Ops:
  7.2 79.7 %all-gather.2.cloned.1.call-start = ((), (), s32[]{:S(2)}) async-start(), calls=%async_computation | async-start | bytes 4718592 | tf_op jit(solution)/shard_map/all_gather | solution.py:19
  7.9 276.0 %all-reduce.2.cloned.1.call-start = ((), (), s32[]{:S(2)}) async-start(), calls=%async_computation.1 | async-start | bytes 4194304 | tf_op jit(solution)/shard_map/psum | solution.py:32
  118.6 26.9 %copy-start = (f32[2048,256]{1,0:T(8,128)S(1)}, f32[2048,256]{1,0:T(8,128)}, u32[]{:S(2)}) copy-start(f32[2048,256]{1,0:T(8,128)} %param.5) | copy-start | bytes 6291460
Sparse Core Ops, SparseCore 0:
  10.2 76.6 all-gather.1
  154.8 129.0 all-reduce.1
where the time goes:
time: 424 us
  waiting for transfers between devices  207 us (49%)
  blocking collectives  165 us (39%)
  matrix products  24.2 us (6%)
  between operations  14.1 us (3%)
  other arithmetic  13.9 us (3%)
    psum x1, waiting for transfers between devices, shards(): lax.psum(lax.dot_general(columns, shares, (((0,), (0,)), ((), ())), prefe...  129 us
    all_gather x1, waiting for transfers between devices, shards(): lax.all_gather(documents, 'cluster', axis=1, tiled=True)  77 us
    psum x1, blocking collectives, shards(): domain_prior = lax.psum(jnp.sum(joint, axis=0), ('cluster', 'dp'))  67.3 us
    psum x1, blocking collectives, shards(): information = lax.psum(jnp.sum(joint * jnp.log(lift)), ('cluster', 'dp'))  62.6 us
    psum x1, blocking collectives, shards(): row_total = lax.psum(jnp.sum(expo, axis=1), 'cluster')  18.2 us
    pmax x1, blocking collectives, shards(): row_max = lax.pmax(jnp.max(scores, axis=1), 'cluster')  16.6 us
    dot_general x1, matrix products, shards(): lax.dot_general(lax.all_gather(documents, 'cluster', axis=1, tiled=True),...  15.1 us
    dot_general x1, matrix products, shards(): lax.dot_general(columns, shares, (((0,), (0,)), ((), ())), preferred_elem...  9.11 us
  transfers between devices with their start and end apart: 2, of which 2 were waited for; matrix products, arithmetic and copies ran while one was open for 0% of the time, Pallas kernels for 0%

commit v1 on v0

--- a/solution.py
+++ b/solution.py
@@ -5,6 +5,11 @@
 from jax.sharding import PartitionSpec as P
 
 E = 1024
+
+
+def one_after_other(array, inner_axis, outer_axis):
+    partial = lax.psum(array, inner_axis)
+    return lax.psum(partial, outer_axis)
 
 
 def shards(documents, centroids, domain_mass):
@@ -38,7 +43,7 @@
     summed = lax.dynamic_slice_in_dim(whole, lax.axis_index("dp") * own_rows, own_rows, 0)
     joint = summed / docs_total
     cluster_mass = jnp.sum(joint, axis=1)
-    domain_prior = lax.psum(jnp.sum(joint, axis=0), ("cluster", "dp"))
+    domain_prior = one_after_other(jnp.sum(joint, axis=0), "dp", "cluster")
     lift = joint / (cluster_mass[:, None] * domain_prior[None, :])
     information = lax.psum(jnp.sum(joint * jnp.log(lift)), ("cluster", "dp"))
     return (lift, information)

time: 424 us -> 412 us (0.972)
  blocking collectives: 165 us -> 152 us
    psum x1 -> x2, blocking collectives: 67.3 us -> 48.6 us  [the longest x1 28.3 us: one_after_other(): partial = lax.psum(array, inner_axis)]
    psum x1, blocking collectives: 62.6 us -> 68.6 us  [shards(): information = lax.psum(jnp.sum(joint * jnp.log(lift)), ('cluster', 'dp'))]
where the time goes in v1:
time: 412 us; the launch traced here: 411 us
  waiting for transfers between devices  207 us (50%)
  blocking collectives  152 us (37%)
  matrix products  24.2 us (6%)
  between operations  14.1 us (3%)
  other arithmetic  13.9 us (3%)
    psum x1, waiting for transfers between devices, shards(): lax.psum(lax.dot_general(columns, shares, (((0,), (0,)), ((), ())), prefe...  129 us
    all_gather x1, waiting for transfers between devices, shards(): lax.all_gather(documents, 'cluster', axis=1, tiled=True)  77 us
    psum x1, blocking collectives, shards(): information = lax.psum(jnp.sum(joint * jnp.log(lift)), ('cluster', 'dp'))  68.6 us
    psum x1, blocking collectives, one_after_other(): partial = lax.psum(array, inner_axis)  28.3 us
    psum x1, blocking collectives, one_after_other(): return lax.psum(partial, outer_axis)  20.3 us
    psum x1, blocking collectives, shards(): row_total = lax.psum(jnp.sum(expo, axis=1), 'cluster')  18.2 us
    pmax x1, blocking collectives, shards(): row_max = lax.pmax(jnp.max(scores, axis=1), 'cluster')  16.6 us
    dot_general x1, matrix products, shards(): lax.dot_general(lax.all_gather(documents, 'cluster', axis=1, tiled=True),...  15.1 us
  transfers between devices with their start and end apart: 2, of which 2 were waited for; matrix products, arithmetic and copies ran while one was open for 0% of the time, Pallas kernels for 0%

profile of v1, /device:TPU:1, one launch (start us, length us, event | category | flops | bytes accessed | tf_op | source)
XLA Modules:
  0.0 411.3 jit_solution(5762625800411717297)
XLA Ops:
  7.2 0.0 all-gather.2.cloned.1.call-start
  7.2 0.7 all-gather.2.cloned.1.call-update
  7.9 0.0 all-reduce.2.cloned.1.call-start
  7.9 1.9 reduce_sum.46
  9.9 77.0 %all-gather.2.cloned.1.call-done = bf16[2048,1024]{1,0:T(8,128)(2,1)} async-done(((bf16[2048,128]{1,0:T(8,128)(2,1)}), bf16[2048,1024]{1,0:T(8,128)(2,1)}) %all-gather.2.cloned.1.call-update) | async-done | bytes 4194320 | tf_op jit(solution)/shard_map/all_gather | solution.py:24
  86.9 15.1 %multiply_reduce_fusion = (f32[2048]{0:T(1024)S(1)}, f32[2048,2048]{0,1:T(8,128)}) fusion(bf16[2048,1024]{1,0:T(8,128)(2,1)} %all-gather.2.cloned.1.call-done, bf16[2048,1024]{1,0:T(8,128)(2,1)} %param.4), kind=kOutput, calls=%fused_computation.2 | convolution fusion | flops 8598321152 | bytes 25174016 | tf_op jit(solution)/shard_map/dot_general | solution.py:23
  102.0 16.6 %pmax.7 = f32[2048]{0:T(1024)S(1)} all-reduce(f32[2048]{0:T(1024)S(1)} %get-tuple-element.6), channel_id=1, replica_groups=mesh['cluster'=8,'dp'=16] {'cluster'}, use_global_device_ids=true, to_apply=%region_1.0 | all-reduce | flops 2048 | bytes 16384 | tf_op jit(solution)/shard_map/pmax | solution.py:31
  118.6 0.0 copy-start
  118.6 8.7 %fusion = f32[2048]{0:T(1024)S(1)} fusion(f32[2048,2048]{0,1:T(8,128)} %get-tuple-element.7, f32[2048]{0:T(1024)S(1)} %pmax.7), kind=kLoop, calls=%fused_computation.3 | loop fusion | flops 12580864 | bytes 16793600 | tf_op jit(solution)/shard_map/reduce_sum | solution.py:33
  127.3 18.2 %psum.35 = f32[2048]{0:T(1024)S(1)} all-reduce(f32[2048]{0:T(1024)S(1)} %fusion), channel_id=1, replica_groups=mesh['cluster'=8,'dp'=16] {'cluster'}, use_global_device_ids=true, to_apply=%region_3.0 | all-reduce | flops 2048 | bytes 16384 | tf_op jit(solution)/shard_map/psum | solution.py:33
  145.5 0.0 copy-done
  145.5 9.1 %fusion.1 = f32[2048,256]{1,0:T(8,128)} fusion(f32[2048,2048]{0,1:T(8,128)} %get-tuple-element.7, f32[2048]{0:T(1024)S(1)} %psum.35, f32[2048]{0:T(1024)S(1)} %pmax.7, f32[2048,256]{1,0:T(8,128)S(1)} %copy-done, f32[2048]{0:T(1024)S(1)} %reduce_sum.46), kind=kOutput, calls=%fused_computation.4 | convolution fusion | flops 2165309440 | bytes 20996096 | tf_op jit(solution)/shard_map/dot_general | solution.py:38
  154.6 0.0 all-reduce.2.cloned.1.call-update
  154.7 129.3 %all-reduce.2.cloned.1.call-done = f32[2048,256]{1,0:T(8,128)} async-done(((f32[2048,256]{1,0:T(8,128)}), f32[2048,256]{1,0:T(8,128)}) %all-reduce.2.cloned.1.call-update) | async-done | bytes 2097168 | tf_op jit(solution)/shard_map/psum | solution.py:37
  283.9 1.0 fusion.4
  284.9 28.3 %psum.37 = f32[256]{0:T(256)S(1)} all-reduce(f32[256]{0:T(256)S(1)} %get-tuple-element.3), channel_id=1, replica_groups=mesh['cluster'=8,'dp'=16] {'dp'}, use_global_device_ids=true, to_apply=%region_8.0 | all-reduce | flops 256 | bytes 2048 | tf_op jit(solution)/shard_map/psum | solution.py:11
  313.2 20.3 %psum.38 = f32[256]{0:T(256)S(1)} all-reduce(f32[256]{0:T(256)S(1)} %psum.37), channel_id=1, replica_groups=mesh['cluster'=8,'dp'=16] {'cluster'}, use_global_device_ids=true, to_apply=%region_9.0 | all-reduce | flops 256 | bytes 2048 | tf_op jit(solution)/shard_map/psum | solution.py:12
  333.5 2.3 multiply_reduce_fusion.1
  335.8 68.6 %psum.39 = f32[]{:T(128)} all-reduce(f32[]{:T(128)} %get-tuple-element.4), channel_id=1, replica_groups=mesh['cluster'=8,'dp'=16] {'cluster','dp'}, use_global_device_ids=true, to_apply=%region_11.0 | all-reduce | flops 1 | bytes 8 | tf_op jit(solution)/shard_map/psum | solution.py:48
Async XLA Ops:
  7.2 79.7 %all-gather.2.cloned.1.call-start = ((), (), s32[]{:S(2)}) async-start(), calls=%async_computation | async-start | bytes 4718592 | tf_op jit(solution)/shard_map/all_gather | solution.py:24
  7.9 276.0 %all-reduce.2.cloned.1.call-start = ((), (), s32[]{:S(2)}) async-start(), calls=%async_computation.1 | async-start | bytes 4194304 | tf_op jit(solution)/shard_map/psum | solution.py:37
  118.6 26.9 %copy-start = (f32[2048,256]{1,0:T(8,128)S(1)}, f32[2048,256]{1,0:T(8,128)}, u32[]{:S(2)}) copy-start(f32[2048,256]{1,0:T(8,128)} %param.5) | copy-start | bytes 6291460
Sparse Core Ops, SparseCore 0:
  10.2 76.6 all-gather.1
  154.8 129.0 all-reduce.1
